TPU v7x, 32 devices: a whole 2x2x4 slice. The times are simulated.
32 devices in a mesh: groups: 2 (over y), ex: 4 (over x, core), par: 4 (over z).
Axes of the slice: x: 2, y: 2, z: 4, core: 2. Of those that a mesh axis runs over, the one named last changes fastest.
Arguments:
- x_in1: bfloat16 [8192, 4096], P(('groups', 'ex'), 'par'), parts along dimension 0, may hold values from -6 to 6
- g_out1: bfloat16 [8192, 11008], P(('groups', 'ex'), 'par'), parts along dimension 0, may hold values from -6 to 6
- x_in2: bfloat16 [8192, 11008], P(('groups', 'ex'), 'par'), parts along dimension 0, may hold values from -6 to 6
- g_out2: bfloat16 [8192, 4096], P(('groups', 'ex'), 'par'), parts along dimension 0, may hold values from -6 to 6
- codebook_d: bfloat16 [16, 128, 64], replicated, may hold values from -0.09375 to 0.09375
- codebook_f: bfloat16 [16, 172, 64], replicated, may hold values from -0.0546875 to 0.0546875
- blocks_d: int32 [2, 32], P(None, 'par'), may hold values from 0 to 15
- blocks_f: int32 [2, 64], P(None, 'par'), may hold values from 0 to 15
- lengths: int32 [8, 16], P(('groups', 'ex')), parts along dimension 0, may hold values from 1 to 256, 1024 in all within a row
- bank: bfloat16 [512, 8192], P('ex', 'par'), may hold values from -0.0078125 to 0.0078125
- query_ids: int32 [1024], replicated, may hold values from 0 to 511
Outputs:
- scores: float32 [128, 1024], P(('groups', 'ex'), 'par'), parts along dimension 0
There are 2 independent parts, one for each index of `groups`. A program takes and returns all parts, laid end to end along the dimension named above; an argument that names none is the same for every part. Nothing has to cross between parts.
Inputs may be any that keep to these rules, and one draw needn't show every extreme that they name: `blocks_d`: every entry names a codebook block. `blocks_f`: every entry names a codebook block. `lengths`: each row sums to 1024; the longest example of each sequence has exactly 256 tokens. `query_ids`: any bank entry, repeats allowed.
All inputs are finite; a program needn't handle non-finite values.
Results may differ from a plain program's by a relative error of at most 0.0051.
Values may be sent and summed in bfloat16 or wider, within the bound.
A program may use at most 64 MiB of HBM per device.

v0:
```python
import jax
import jax.numpy as jnp
from jax import lax
from jax.sharding import PartitionSpec as P


def codebook_matrix(picks, codebook):
    count = codebook.shape[0]
    onehot = (picks[:, None] == jnp.arange(count, dtype=jnp.int32)[None, :]).astype(jnp.bfloat16)
    flat = codebook.reshape(count, codebook.shape[1] * codebook.shape[2])
    chosen = jnp.dot(onehot, flat, preferred_element_type=jnp.float32).astype(jnp.bfloat16)
    return chosen.reshape(picks.shape[0] * codebook.shape[1], codebook.shape[2])


def on_device(
    x_in1,
    g_out1,
    x_in2,
    g_out2,
    codebook_d,
    codebook_f,
    blocks_d,
    blocks_f,
    lengths,
    bank,
    query_ids,
):
    rank = codebook_d.shape[2]
    tok_count = x_in1.shape[0]
    proj_g1 = jnp.dot(
        g_out1, codebook_matrix(blocks_f[0], codebook_f), preferred_element_type=jnp.float32
    )
    proj_x1 = jnp.dot(
        x_in1, codebook_matrix(blocks_d[0], codebook_d), preferred_element_type=jnp.float32
    )
    proj_g2 = jnp.dot(
        g_out2, codebook_matrix(blocks_d[1], codebook_d), preferred_element_type=jnp.float32
    )
    proj_x2 = jnp.dot(
        x_in2, codebook_matrix(blocks_f[1], codebook_f), preferred_element_type=jnp.float32
    )
    par_count = lax.axis_size("par")
    width = 2 * rank // par_count
    first = lax.axis_index("par") * width
    layer = first // rank
    offset = first % rank
    partial_rows = jnp.concatenate([proj_g1, proj_x1, proj_g2, proj_x2], axis=1)
    rows = lax.psum(partial_rows, "par").astype(jnp.bfloat16)
    out_side = lax.dynamic_slice_in_dim(rows, layer * 2 * rank + offset, width, 1)
    in_side = lax.dynamic_slice_in_dim(rows, layer * 2 * rank + rank, rank, 1)
    lens = lengths[0]
    ends = jnp.cumsum(lens)
    starts = ends - lens
    position = jnp.arange(tok_count, dtype=jnp.int32)[:, None]
    member = ((position >= starts[None, :]) & (position < ends[None, :])).astype(jnp.bfloat16)
    count_ex = lens.shape[0]
    weighted = (member[:, :, None] * out_side[:, None, :]).reshape(tok_count, count_ex * width)
    outer = lax.dot_general(
        weighted, in_side, (((0,), (0,)), ((), ())), preferred_element_type=jnp.float32
    )
    grads = outer.reshape(count_ex, width * rank).astype(jnp.bfloat16)
    piece = lax.all_gather(bank, "ex", axis=0, tiled=True)
    against = lax.dot_general(
        grads, piece, (((1,), (1,)), ((), ())), preferred_element_type=jnp.float32
    )
    entry = jnp.arange(piece.shape[0], dtype=jnp.int32)
    select = (query_ids[None, :] == entry[:, None]).astype(jnp.float32)
    partial_scores = jnp.dot(against, select, precision=lax.Precision.HIGHEST)
    return lax.psum_scatter(partial_scores, "par", scatter_dimension=1, tiled=True)


def solution(mesh):
    return jax.shard_map(
        on_device,
        mesh=mesh,
        in_specs=(
            P(("groups", "ex"), "par"),
            P(("groups", "ex"), "par"),
            P(("groups", "ex"), "par"),
            P(("groups", "ex"), "par"),
            P(),
            P(),
            P(None, "par"),
            P(None, "par"),
            P(("groups", "ex"), None),
            P("ex", "par"),
            P(),
        ),
        out_specs=P(("groups", "ex"), "par"),
        check_vma=False,
    )
```

profile of v0, /device:TPU:0, one launch (start us, length us, event | category | flops | bytes accessed | tf_op | source)
XLA Modules:
  0.0 103.4 jit_solution(10102008912007583445)
XLA Ops:
  6.5 0.0 copy-start
  6.5 0.0 copy-start.5
  6.5 0.0 copy-start.4
  6.5 0.0 copy-start.6
  6.5 0.0 all-gather.2.cloned.1.call-start
  6.6 0.7 all-gather.2.cloned.1.call-update
  7.3 0.0 reduce-scatter.2.cloned.1.call-start
  7.3 1.4 %copy.15 = bf16[16,172,64]{2,1,0:T(8,128)(2,1)S(1)} copy(bf16[16,172,64]{1,2,0:T(8,128)(2,1)} %param.16) | data formatting | bytes 704512 | tf_op args[5]
  8.7 0.5 reshape.85
  9.2 0.0 copy-done.5
  9.2 0.0 copy-done.4
  9.2 0.3 copy.16
  9.5 0.5 reshape.87
  10.0 0.0 copy-done.6
  10.0 0.2 convolution_convert_fusion.2
  10.3 0.2 reshape.89
  10.5 0.2 convolution_convert_fusion.3
  10.7 0.2 reshape.88
  11.0 0.0 copy-start.1
  11.0 0.3 convolution_convert_fusion
  11.3 0.0 copy-done
  11.3 1.5 %convolution_bitcast_fusion.1 = f32[1024,64]{0,1:T(8,128)} fusion(bf16[1024,64]{1,0:T(8,128)(2,1)S(1)} %reshape.89, bf16[1024,1024]{1,0:T(8,128)(2,1)S(1)} %copy-done), kind=kOutput, calls=%fused_computation.7 | convolution fusion | flops 134217728 | bytes 2490368 | tf_op jit(solution)/shard_map/dot_general | solution.py:36
  12.8 0.0 copy-done.1
  12.8 1.5 %convolution_bitcast_fusion.2 = f32[1024,64]{0,1:T(8,128)} fusion(bf16[1024,64]{1,0:T(8,128)(2,1)S(1)} %reshape.88, bf16[1024,1024]{1,0:T(8,128)(2,1)S(1)} %copy-done.1), kind=kOutput, calls=%fused_computation.8 | convolution fusion | flops 134217728 | bytes 2490368 | tf_op jit(solution)/shard_map/dot_general | solution.py:33
  14.3 1.1 %convolution_convert_fusion.1 = bf16[16,11008]{1,0:T(8,128)(2,1)} fusion(bf16[16,11008]{1,0:T(8,128)(2,1)S(1)} %reshape.85, s32[16]{0:T(128)S(1)} %get-tuple-element.5), kind=kOutput, calls=%fused_computation.1 | convolution fusion | flops 5812480 | bytes 704576 | tf_op jit(solution)/shard_map/dot_general | solution.py:11
  15.3 0.4 reshape.90
  15.7 1.4 %reshape.86 = bf16[2752,64]{1,0:T(8,128)(2,1)S(1)} reshape(bf16[16,11008]{1,0:T(8,128)(2,1)} %convolution_convert_fusion.1) | data formatting | bytes 704512 | tf_op jit(solution)/shard_map/reshape | solution.py:12
  17.1 4.2 %convolution_bitcast_fusion = f32[1024,64]{0,1:T(8,128)S(1)} fusion(bf16[2752,64]{1,0:T(8,128)(2,1)S(1)} %reshape.90, bf16[1024,2752]{0,1:T(8,128)(2,1)} %param.13), kind=kOutput, calls=%fused_computation.6 | convolution fusion | flops 360710144 | bytes 6250496 | tf_op jit(solution)/shard_map/dot_general | solution.py:39
  21.3 0.0 copy-start.2
  21.3 0.0 copy-start.3
  21.3 3.8 %convolution_bitcast_fusion.3 = f32[1024,64]{0,1:T(8,128)S(1)} fusion(bf16[2752,64]{1,0:T(8,128)(2,1)S(1)} %reshape.86, bf16[1024,2752]{0,1:T(8,128)(2,1)} %param.12), kind=kOutput, calls=%fused_computation.9 | convolution fusion | flops 360710144 | bytes 6250496 | tf_op jit(solution)/shard_map/dot_general | solution.py:30
  25.1 0.0 copy-done.2
  25.1 0.0 copy-done.3
  25.1 0.0 copy-start.7
  25.1 0.1 pad_maximum_fusion
  25.2 0.5 copy-done.7
  25.8 0.1 copy.14
  25.9 0.1 reduce
  26.0 45.5 %all-reduce.1 = bf16[1024,256]{0,1:T(8,128)(2,1)} all-reduce(f32[1024,256]{0,1:T(8,128)S(1)} %pad_maximum_fusion), channel_id=1, replica_groups=mesh['groups'=2,'ex'=4,'par'=4] {'par'}, use_global_device_ids=true, to_apply=%region_1.2 | all-reduce | flops 262144 | bytes 1572864 | tf_op jit(solution)/shard_map/psum | solution.py:48
  71.5 0.9 constant_dynamic-slice_fusion
  72.4 0.1 fusion.4
  72.5 0.1 broadcast_multiply_fusion
  72.6 0.0 copy-start.8
  72.6 1.4 %convolution_convert_fusion.4 = bf16[512,64]{0,1:T(8,128)(2,1)S(1)} fusion(bf16[1024,512]{0,1:T(8,128)(2,1)S(1)} %bitcast.40, bf16[1024,256]{0,1:T(8,128)(2,1)} %all-reduce.1, s32[]{:T(128)S(6)} %select_n.20), kind=kOutput, calls=%fused_computation.10 | convolution fusion | flops 67141632 | bytes 1245188 | tf_op jit(solution)/shard_map/dot_general | solution.py:58
  74.0 0.1 copy.17
  74.1 0.2 convert_element_type.40
  74.3 0.0 all-gather.2.cloned.1.call-done
  74.3 2.2 %fusion.11 = f32[16,512]{1,0:T(8,128)S(1)} fusion(bf16[16,2048]{1,0:T(8,128)(2,1)S(1)} %convert_element_type.40, bf16[512,2048]{1,0:T(8,128)(2,1)} %all-gather.2.cloned.1.call-done), kind=kOutput, calls=%fused_computation.35 | convolution fusion | flops 33554432 | bytes 2195456 | tf_op jit(solution)/shard_map/dot_general | solution.py:63
  76.6 0.0 copy-done.8
  76.6 1.4 %fusion = f32[16,1024]{1,0:T(8,128)} fusion(f32[16,512]{1,0:T(8,128)S(1)} %fusion.11, s32[1024]{0:T(1024)S(1)} %copy-done.8), kind=kOutput, calls=%fused_computation.5 | convolution fusion | flops 101187584 | bytes 102400 | tf_op jit(solution)/shard_map/dot_general | solution.py:68
  77.9 0.0 reduce-scatter.2.cloned.1.call-update
  78.0 18.6 %reduce-scatter.2.cloned.1.call-done = f32[16,256]{1,0:T(8,128)} async-done(((f32[16,1024]{1,0:T(8,128)}), f32[16,256]{1,0:T(8,128)}) %reduce-scatter.2.cloned.1.call-update) | async-done | bytes 16400 | tf_op jit(solution)/shard_map/reduce_scatter | solution.py:69
  (4 shorter events, 0.1 us)
Async XLA Ops:
  6.5 4.8 %copy-start = (bf16[1024,1024]{1,0:T(8,128)(2,1)S(1)}, bf16[1024,1024]{1,0:T(8,128)(2,1)}, u32[]{:S(2)}) copy-start(bf16[1024,1024]{1,0:T(8,128)(2,1)} %param.14) | copy-start | bytes 6291460
  6.5 2.7 %copy-start.5 = (s32[2,16]{1,0:T(2,128)S(1)}, s32[2,16]{1,0:T(2,128)}, u32[]{:S(2)}) copy-start(s32[2,16]{1,0:T(2,128)} %param.18) | copy-start | bytes 388
  6.5 2.7 %copy-start.4 = (bf16[16,128,64]{1,2,0:T(8,128)(2,1)S(1)}, bf16[16,128,64]{1,2,0:T(8,128)(2,1)}, u32[]{:S(2)}) copy-start(bf16[16,128,64]{1,2,0:T(8,128)(2,1)} %param.15) | copy-start | bytes 786436
  6.5 3.5 %copy-start.6 = (s32[2,8]{1,0:T(2,128)S(1)}, s32[2,8]{1,0:T(2,128)}, u32[]{:S(2)}) copy-start(s32[2,8]{1,0:T(2,128)} %param.17) | copy-start | bytes 196
  6.5 67.8 %all-gather.2.cloned.1.call-start = ((), (), s32[]{:S(2)}) async-start(), calls=%async_computation.1 | async-start | bytes 2621440 | tf_op jit(solution)/shard_map/all_gather | solution.py:62
  7.3 89.3 %reduce-scatter.2.cloned.1.call-start = ((), (), s32[]{:S(2)}) async-start(), calls=%async_computation.2 | async-start | bytes 81920 | tf_op jit(solution)/shard_map/reduce_scatter | solution.py:69
  11.0 1.8 %copy-start.1 = (bf16[1024,1024]{1,0:T(8,128)(2,1)S(1)}, bf16[1024,1024]{1,0:T(8,128)(2,1)}, u32[]{:S(2)}) copy-start(bf16[1024,1024]{1,0:T(8,128)(2,1)} %param.11) | copy-start | bytes 6291460
  21.3 3.8 %copy-start.2 = (f32[1024,64]{0,1:T(8,128)S(1)}, f32[1024,64]{0,1:T(8,128)}, u32[]{:S(2)}) copy-start(f32[1024,64]{0,1:T(8,128)} %convolution_bitcast_fusion.1) | copy-start | bytes 786436
  21.3 3.8 %copy-start.3 = (f32[1024,64]{0,1:T(8,128)S(1)}, f32[1024,64]{0,1:T(8,128)}, u32[]{:S(2)}) copy-start(f32[1024,64]{0,1:T(8,128)} %convolution_bitcast_fusion.2) | copy-start | bytes 786436
  25.1 0.7 copy-start.7
  72.6 4.0 %copy-start.8 = (s32[1024]{0:T(1024)S(1)}, s32[1024]{0:T(1024)}, u32[]{:S(2)}) copy-start(s32[1024]{0:T(1024)} %param.21) | copy-start | bytes 12292
Sparse Core Ops, SparseCore 0:
  8.9 25.2 all-gather.1
  78.1 18.4 reduce-scatter.1
where the time goes:
time: 104 us; the launch traced here: 103 us
  blocking collectives  45.5 us (44%)
  waiting for transfers between devices  19.3 us (19%)
  matrix products  17.7 us (17%)
  between operations  13.6 us (13%)
  local copies, waits for them, and re-layouts  6.8 us (7%)
    psum x1, blocking collectives, on_device(): rows = lax.psum(partial_rows, 'par').astype(jnp.bfloat16)  45.5 us
    reduce_scatter x1, waiting for transfers between devices, on_device(): lax.psum_scatter(partial_scores, 'par', scatter_dimension=1, tiled=True)  18.6 us
    dot_general x1, matrix products, on_device(): jnp.dot(x_in2, codebook_matrix(blocks_f[1], codebook_f), preferred_elemen...  4.16 us
    dot_general x1, matrix products, on_device(): jnp.dot(g_out1, codebook_matrix(blocks_f[0], codebook_f), preferred_eleme...  3.77 us
    unnamed x20, local copies, waits for them, and re-layouts  2.27 us
    reshape x4, local copies, waits for them, and re-layouts, codebook_matrix(): return chosen.reshape(picks.shape[0] * codebook.shape[1], codebook.shape[2])  2.26 us
    dot_general x1, matrix products, on_device(): lax.dot_general(grads, piece, (((1,), (1,)), ((), ())), preferred_element...  2.23 us
  transfers between devices with their start and end apart: 2, of which 1 were waited for; matrix products, arithmetic and copies ran while one was open for 20% of the time, Pallas kernels for 0%

commit v1 on v0

v1 whole, which is shorter than its diff:
```python
import functools

import jax
import jax.numpy as jnp
from jax import lax
from jax.experimental import pallas as pl
from jax.experimental.pallas import tpu as pltpu
from jax.sharding import PartitionSpec as P

MESH = pl.DeviceIdType.MESH
LAYERS = 2
BANK_PIECES = 4


def kernel(
    par_count,
    ex_count,
    chunks,
    x1_ref,
    g1_ref,
    x2_ref,
    g2_ref,
    cbd_ref,
    cbf_ref,
    bd_ref,
    bf_ref,
    len_ref,
    bank_ref,
    qid_ref,
    out_ref,
    wide_s,
    narrow_s,
    tall,
    pw,
    pn,
    stage,
    recv,
    own,
    rows,
    turned,
    weighted,
    outer,
    grads,
    banks,
    onehot,
    part_s,
    part_r,
    in_sem,
    send_sem,
    recv_sem,
    row_send,
    row_recv,
    bank_local,
    bank_send,
    bank_recv,
    fwd_send,
    fwd_recv,
    sc_send,
    sc_recv,
):
    rank = cbd_ref.shape[2]
    group = par_count // LAYERS
    per = chunks // group
    size = wide_s.shape[2]
    width = rank // group
    count_ex = len_ref.shape[1]
    me = lax.axis_index("par")
    ex = lax.axis_index("ex")
    layer = me // group
    place = lax.rem(me, group)
    core = lax.rem(ex, 2)
    sibling = ex + 1 - 2 * core
    piece_rows = banks.shape[2]

    def order(step):
        far = step < chunks
        inner = lax.rem(step, chunks)
        l = jnp.where(far, 1 - layer, layer)
        shift = jnp.where(far, place * per, (place + 1) * per)
        return l, lax.rem(inner + shift, chunks)

    wides = (g1_ref, x2_ref)
    narrows = (x1_ref, g2_ref)

    def fetch(l, c):
        span = pl.ds(pl.multiple_of(c * size, size), size)
        pltpu.make_async_copy(wides[l].at[span, :], wide_s.at[l, c], in_sem.at[l, c, 0]).start()
        pltpu.make_async_copy(narrows[l].at[span, :], narrow_s.at[l, c], in_sem.at[l, c, 1]).start()

    for mine in range(LAYERS):
        @pl.when(layer == mine)
        def _(mine=mine):
            for step in range(2 * chunks):
                fetch((1 - mine) if step < chunks else mine, order(step)[1])

    local_bank = []
    for i in range(BANK_PIECES):
        span = pl.ds(i * piece_rows, piece_rows)
        copy = pltpu.make_async_copy(bank_ref.at[span, :], banks.at[ex, i], bank_local.at[i])
        copy.start()
        local_bank.append(copy)

    barrier = pltpu.get_barrier_semaphore()
    for k in range(1, par_count):
        pl.semaphore_signal(barrier, inc=1, device_id={"par": lax.rem(me + k, par_count)}, device_id_type=MESH)
    for k in range(1, ex_count // 2):
        pl.semaphore_signal(barrier, inc=1, device_id={"ex": lax.rem(ex + 2 * k, ex_count)}, device_id_type=MESH)
    pl.semaphore_signal(barrier, inc=1, device_id={"ex": sibling}, device_id_type=MESH)

    depth = cbf_ref.shape[1]
    high = tall.shape[0]
    for l in range(LAYERS):
        fill = jnp.zeros((depth, rank), jnp.float32)
        for b in range(bf_ref.shape[1]):
            block = cbf_ref[bf_ref[l, b]].astype(jnp.float32)
            both = [block, fill] if l == 0 else [fill, block]
            tall[b * depth:(b + 1) * depth, :] = jnp.concatenate(both, axis=1)
        pw[l] = tall[...].astype(jnp.bfloat16)
        deep = cbd_ref.shape[1]
        fill = jnp.zeros((deep, rank), jnp.float32)
        for b in range(bd_ref.shape[1]):
            block = cbd_ref[bd_ref[l, b]].astype(jnp.float32)
            both = [fill, block] if l == 0 else [block, fill]
            pn[l, b * deep:(b + 1) * deep, :] = jnp.concatenate(both, axis=1).astype(jnp.bfloat16)

    pl.semaphore_wait(barrier, par_count - 1 + ex_count // 2)

    for i in range(BANK_PIECES):
        span = pl.ds(i * piece_rows, piece_rows)
        for k in range(1, ex_count // 2):
            pltpu.make_async_remote_copy(
                bank_ref.at[span, :], banks.at[ex, i], bank_send.at[k, i], bank_recv.at[ex, i],
                device_id={"ex": lax.rem(ex + 2 * k, ex_count)}, device_id_type=MESH,
            ).start()
    for i in range(BANK_PIECES):
        span = pl.ds(i * piece_rows, piece_rows)
        pltpu.make_async_remote_copy(
            bank_ref.at[span, :], banks.at[ex, i], bank_send.at[0, i], bank_recv.at[ex, i],
            device_id={"ex": sibling}, device_id_type=MESH,
        ).start()

    def project(l, c):
        span = pl.ds(0, size)
        pltpu.make_async_copy(g1_ref.at[span, :], wide_s.at[l, c], in_sem.at[l, c, 0]).wait()
        pltpu.make_async_copy(x1_ref.at[span, :], narrow_s.at[l, c], in_sem.at[l, c, 1]).wait()
        return jnp.dot(wide_s[l, c], pw[l], preferred_element_type=jnp.float32) + jnp.dot(
            narrow_s[l, c], pn[l], preferred_element_type=jnp.float32
        )

    def partial_copy(step, l, c):
        return pltpu.make_async_remote_copy(
            stage.at[step], recv.at[me, lax.rem(c, per)], send_sem.at[step], recv_sem.at[me, lax.rem(c, per)],
            device_id={"par": l * group + c // per}, device_id_type=MESH,
        )

    sent = 2 * chunks - per

    def send_step(step, carry):
        l, c = order(step)
        stage[step] = project(l, c).astype(jnp.bfloat16)
        partial_copy(step, l, c).start()
        return carry

    lax.fori_loop(0, sent, send_step, 0)

    def keep_step(j, carry):
        own[j] = project(layer, place * per + j)
        return carry

    lax.fori_loop(0, per, keep_step, 0)

    entry = lax.broadcasted_iota(jnp.int32, onehot.shape, 0)
    onehot[...] = (entry == qid_ref[...]).astype(jnp.float32).astype(jnp.bfloat16)
    lane = lax.broadcasted_iota(jnp.int32, (count_ex, size), 1)
    which = lax.broadcasted_iota(jnp.int32, (count_ex, size), 0)
    starts = jnp.zeros((count_ex, size), jnp.int32)
    ends = jnp.zeros((count_ex, size), jnp.int32)
    total = jnp.int32(0)
    for e in range(count_ex):
        starts = jnp.where(which == e, total, starts)
        total = total + len_ref[0, e]
        ends = jnp.where(which == e, total, ends)
    outer[...] = jnp.zeros_like(outer)

    def bank_forward(i):
        for k in range(1, ex_count // 2):
            source = lax.rem(ex + 2 * k, ex_count)
            pltpu.make_async_remote_copy(
                banks.at[source, i], banks.at[source, i], bank_send.at[k, i], bank_recv.at[source, i],
                device_id={"ex": source}, device_id_type=MESH,
            ).wait_recv()
            pltpu.make_async_remote_copy(
                banks.at[source, i], banks.at[source, i], fwd_send.at[k, i], fwd_recv.at[source, i],
                device_id={"ex": sibling}, device_id_type=MESH,
            ).start()

    def add_outer(c):
        held = rows[c]
        turned[...] = held.astype(jnp.float32).T
        token = lane + c * size
        member = ((token >= starts) & (token < ends)).astype(jnp.float32)
        slab = turned[pl.ds(pl.multiple_of(place * width, width), width), :]
        for a in range(width):
            weighted[a * count_ex:(a + 1) * count_ex, :] = (member * slab[a:a + 1, :]).astype(jnp.bfloat16)
        outer[...] += jnp.dot(weighted[...], held, preferred_element_type=jnp.float32)

    def row_copy(k, j):
        c = place * per + j
        return pltpu.make_async_remote_copy(
            rows.at[c], rows.at[c], row_send.at[k, j], row_recv.at[c],
            device_id={"par": layer * group + lax.rem(place + k, group)}, device_id_type=MESH,
        )

    done = 0
    for j in range(per):
        acc = own[j]
        for k in range(1, par_count):
            source = lax.rem(me + k, par_count)
            pltpu.make_async_remote_copy(
                stage.at[0], recv.at[source, j], send_sem.at[0], recv_sem.at[source, j],
                device_id={"par": source}, device_id_type=MESH,
            ).wait_recv()
            acc = acc + recv[source, j].astype(jnp.float32)
        c = place * per + j
        rows[c] = acc.astype(jnp.bfloat16)
        for k in range(1, group):
            row_copy(k, j).start()
        goal = BANK_PIECES * (j + 1) // per
        for i in range(done, goal):
            bank_forward(i)
        done = goal
        add_outer(c)
    for k in range(1, group):
        for j in range(per):
            c = lax.rem(place + k, group) * per + j
            pltpu.make_async_remote_copy(
                rows.at[c], rows.at[c], row_send.at[k, j], row_recv.at[c],
                device_id={"par": layer * group + lax.rem(place + k, group)}, device_id_type=MESH,
            ).wait_recv()
            add_outer(c)

    upper = lax.broadcasted_iota(jnp.int32, (count_ex, 2 * rank), 1) >= rank
    rolled = pltpu.roll(outer[...], rank, 1)
    for pair in range(width // 2):
        even = rolled[2 * pair * count_ex:(2 * pair + 1) * count_ex, :]
        odd = outer[(2 * pair + 1) * count_ex:(2 * pair + 2) * count_ex, :]
        grads[:, 2 * rank * pair:2 * rank * (pair + 1)] = jnp.where(upper, odd, even).astype(jnp.bfloat16)

    for copy in local_bank:
        copy.wait()
    for i in range(BANK_PIECES):
        pltpu.make_async_remote_copy(
            banks.at[sibling, i], banks.at[sibling, i], bank_send.at[0, i], bank_recv.at[sibling, i],
            device_id={"ex": sibling}, device_id_type=MESH,
        ).wait_recv()
        for k in range(1, ex_count // 2):
            source = lax.rem(sibling + 2 * k, ex_count)
            pltpu.make_async_remote_copy(
                banks.at[source, i], banks.at[source, i], fwd_send.at[k, i], fwd_recv.at[source, i],
                device_id={"ex": sibling}, device_id_type=MESH,
            ).wait_recv()

    every = banks[...].reshape(onehot.shape[0], grads.shape[1])
    against = lax.dot_general(grads[...], every, (((1,), (1,)), ((), ())), preferred_element_type=jnp.float32)
    high_part = against.astype(jnp.bfloat16)
    low_part = (against - high_part.astype(jnp.float32)).astype(jnp.bfloat16)
    both = jnp.concatenate([high_part, low_part], axis=0)
    picked = jnp.dot(both, onehot[...], preferred_element_type=jnp.float32)
    picked = picked[:count_ex] + picked[count_ex:]
    share = part_s.shape[2]
    for d in range(par_count):
        part_s[d] = picked[:, d * share:(d + 1) * share]
    for k in range(1, par_count):
        target = lax.rem(me + k, par_count)
        pltpu.make_async_remote_copy(
            part_s.at[target], part_r.at[me], sc_send.at[k], sc_recv.at[me],
            device_id={"par": target}, device_id_type=MESH,
        ).start()
    result = part_s[me]
    for k in range(1, par_count):
        source = lax.rem(me + k, par_count)
        pltpu.make_async_remote_copy(
            part_s.at[source], part_r.at[source], sc_send.at[k], sc_recv.at[source],
            device_id={"par": source}, device_id_type=MESH,
        ).wait_recv()
        result = result + part_r[source]
    out_ref[...] = result

    def sent_step(step, carry):
        l, c = order(step)
        partial_copy(step, l, c).wait_send()
        return carry

    lax.fori_loop(0, sent, sent_step, 0)
    for k in range(1, group):
        for j in range(per):
            row_copy(k, j).wait_send()
    for i in range(BANK_PIECES):
        span = pl.ds(i * piece_rows, piece_rows)
        for k in range(ex_count // 2):
            pltpu.make_async_remote_copy(
                bank_ref.at[span, :], banks.at[ex, i], bank_send.at[k, i], bank_recv.at[ex, i],
                device_id={"ex": sibling}, device_id_type=MESH,
            ).wait_send()
        for k in range(1, ex_count // 2):
            source = lax.rem(ex + 2 * k, ex_count)
            pltpu.make_async_remote_copy(
                banks.at[source, i], banks.at[source, i], fwd_send.at[k, i], fwd_recv.at[source, i],
                device_id={"ex": sibling}, device_id_type=MESH,
            ).wait_send()
    for k in range(1, par_count):
        target = lax.rem(me + k, par_count)
        pltpu.make_async_remote_copy(
            part_s.at[target], part_r.at[me], sc_send.at[k], sc_recv.at[me],
            device_id={"par": target}, device_id_type=MESH,
        ).wait_send()


def on_device(x_in1, g_out1, x_in2, g_out2, codebook_d, codebook_f, blocks_d, blocks_f, lengths, bank, query_ids):
    par_count = lax.axis_size("par")
    ex_count = lax.axis_size("ex")
    tokens, slim = x_in1.shape
    broad = g_out1.shape[1]
    rank = codebook_d.shape[2]
    group = par_count // LAYERS
    chunks = group * max(1, 4 // group)
    per = chunks // group
    size = tokens // chunks
    count_ex = lengths.shape[1]
    width = rank // group
    entries, dims = bank.shape
    queries = query_ids.shape[0]
    share = queries // par_count
    half = ex_count // 2
    bf16, f32 = jnp.bfloat16, jnp.float32
    dma = pltpu.SemaphoreType.DMA
    hbm = pl.BlockSpec(memory_space=pl.ANY)
    vmem = pl.BlockSpec(memory_space=pltpu.VMEM)
    smem = pl.BlockSpec(memory_space=pltpu.SMEM)
    return pl.pallas_call(
        functools.partial(kernel, par_count, ex_count, chunks),
        out_shape=jax.ShapeDtypeStruct((count_ex, share), f32),
        in_specs=[hbm, hbm, hbm, hbm, vmem, vmem, smem, smem, smem, hbm, vmem],
        out_specs=vmem,
        scratch_shapes=[
            pltpu.VMEM((LAYERS, chunks, size, broad), bf16),
            pltpu.VMEM((LAYERS, chunks, size, slim), bf16),
            pltpu.VMEM((broad, 2 * rank), f32),
            pltpu.VMEM((LAYERS, broad, 2 * rank), bf16),
            pltpu.VMEM((LAYERS, slim, 2 * rank), bf16),
            pltpu.VMEM((2 * chunks - per, size, 2 * rank), bf16),
            pltpu.VMEM((par_count, per, size, 2 * rank), bf16),
            pltpu.VMEM((per, size, 2 * rank), f32),
            pltpu.VMEM((chunks, size, 2 * rank), bf16),
            pltpu.VMEM((2 * rank, size), f32),
            pltpu.VMEM((width * count_ex, size), bf16),
            pltpu.VMEM((width * count_ex, 2 * rank), f32),
            pltpu.VMEM((count_ex, dims), bf16),
            pltpu.VMEM((ex_count, BANK_PIECES, entries // BANK_PIECES, dims), bf16),
            pltpu.VMEM((ex_count * entries, queries), bf16),
            pltpu.VMEM((par_count, count_ex, share), f32),
            pltpu.VMEM((par_count, count_ex, share), f32),
            dma((LAYERS, chunks, 2)),
            dma((2 * chunks - per,)),
            dma((par_count, per)),
            dma((group, per)),
            dma((chunks,)),
            dma((BANK_PIECES,)),
            dma((half, BANK_PIECES)),
            dma((ex_count, BANK_PIECES)),
            dma((half, BANK_PIECES)),
            dma((ex_count, BANK_PIECES)),
            dma((par_count,)),
            dma((par_count,)),
        ],
        compiler_params=pltpu.CompilerParams(
            collective_id=0, has_side_effects=True, vmem_limit_bytes=56 * 1024 * 1024
        ),
    )(
        x_in1, g_out1, x_in2, g_out2, codebook_d, codebook_f, blocks_d, blocks_f, lengths, bank,
        query_ids.reshape(1, queries),
    )


def solution(mesh):
    return jax.shard_map(
        on_device,
        mesh=mesh,
        in_specs=(
            P(("groups", "ex"), "par"),
            P(("groups", "ex"), "par"),
            P(("groups", "ex"), "par"),
            P(("groups", "ex"), "par"),
            P(),
            P(),
            P(None, "par"),
            P(None, "par"),
            P(("groups", "ex"), None),
            P("ex", "par"),
            P(),
        ),
        out_specs=P(("groups", "ex"), "par"),
        check_vma=False,
    )
```

time: 104 us -> 52.1 us (0.50)
  blocking collectives: 45.5 us -> 0 us
  Pallas kernels: 0 us -> 29.2 us
  waiting for transfers between devices: 19.3 us -> 0 us
  matrix products: 17.7 us -> 0 us
  local copies, waits for them, and re-layouts: 6.8 us -> 22.2 us
  between operations: 13.6 us -> 0.01 us
    psum x1 -> x0, blocking collectives: 45.5 us -> none  [on_device(): rows = lax.psum(partial_rows, 'par').astype(jnp.bfloat16)]
    pallas_call x0 -> x1, Pallas kernels: none -> 29.2 us  [on_device(): pl.pallas_call(functools.partial(kernel, par_count, ex_count, chunks), ou...]
    unnamed x20 -> x5, local copies, waits for them, and re-layouts: 2.27 us -> 22.2 us
    reduce_scatter x1 -> x0, waiting for transfers between devices: 18.6 us -> none  [on_device(): lax.psum_scatter(partial_scores, 'par', scatter_dimension=1, tiled=True)]
    dot_general x11 -> x0, matrix products: 17.7 us -> none  [the longest x1 4.16 us: on_device(): jnp.dot(x_in2, codebook_matrix(blocks_f[1], codebook_f), preferred_elemen...]
    reshape x7 -> x0, local copies, waits for them, and re-layouts: 3.3 us -> none  [the longest x4 2.26 us: codebook_matrix(): return chosen.reshape(picks.shape[0] * codebook.shape[1], codebook.shape[2])]
  transfers between devices with their start and end apart: 2 -> 0, of which waited for: 1 -> 0; matrix products, arithmetic and copies ran while one was open for 20% -> 0% of each run, Pallas kernels for 0% -> 0%
where the time goes in v1:
time: 52.1 us; the launch traced here: 51.4 us
  Pallas kernels  29.2 us (56%)
  local copies, waits for them, and re-layouts  22.2 us (43%)
    pallas_call x1, Pallas kernels, on_device(): pl.pallas_call(functools.partial(kernel, par_count, ex_count, chunks), ou...  29.2 us
    unnamed x5, local copies, waits for them, and re-layouts  22.2 us

profile of v1, /device:TPU:0, one launch (start us, length us, event | category | flops | bytes accessed | tf_op | source)
XLA Modules:
  0.0 51.4 jit_solution(2090043253592290766)
XLA Ops:
  0.0 2.0 %copy.14.cbd_ref = bf16[16,128,64]{2,1,0:T(8,128)(2,1)} copy(bf16[16,128,64]{1,2,0:T(8,128)(2,1)} %param.15) | data formatting | bytes 524288 | tf_op args[4]
  2.0 2.2 %copy.15.cbf_ref = bf16[16,172,64]{2,1,0:T(8,128)(2,1)} copy(bf16[16,172,64]{1,2,0:T(8,128)(2,1)} %param.16) | data formatting | bytes 704512 | tf_op args[5]
  4.2 8.3 %copy.12.g1_ref = bf16[1024,2752]{1,0:T(8,128)(2,1)} copy(bf16[1024,2752]{0,1:T(8,128)(2,1)} %param.12) | data formatting | bytes 11272192 | tf_op args[1]
  12.5 8.4 %copy.13.x2_ref = bf16[1024,2752]{1,0:T(8,128)(2,1)} copy(bf16[1024,2752]{0,1:T(8,128)(2,1)} %param.13) | data formatting | bytes 11272192 | tf_op args[2]
  20.9 29.2 %shard_map.109 = f32[16,256]{1,0:T(8,128)} custom-call(bf16[1024,1024]{1,0:T(8,128)(2,1)} %x1_ref.1, bf16[1024,2752]{1,0:T(8,128)(2,1)} %copy.12.g1_ref, bf16[1024,2752]{1,0:T(8,128)(2,1)} %copy.13.x2_ref, bf16[1024,1024]{1,0:T(8,128)(2,1)} %g2_ref.1, bf16[16,128,64]{2,1,0:T(8,128)(2,1)} %copy.14.cbd_ref, bf16[16,172,64]{2,1,0:T(8,128)(2,1)} %copy.15.cbf_ref, ...), custom_call_target="tpu_custom_call" | custom-call | tf_op jit(solution)/shard_map/pallas_call | solution.py:340
  50.1 1.3 %copy.17 = f32[16,256]{1,0:T(8,128)} copy(f32[16,256]{1,0:T(8,128)} %shard_map.109) | data formatting | bytes 32768

commit v2 on v1

--- a/solution.py
+++ b/solution.py
@@ -37,7 +37,7 @@
     recv,
     own,
     rows,
-    turned,
+    twice,
     weighted,
     outer,
     grads,
@@ -58,10 +58,10 @@
     sc_send,
     sc_recv,
 ):
-    rank = cbd_ref.shape[2]
+    rank = cbd_ref.shape[1]
     group = par_count // LAYERS
     per = chunks // group
-    size = wide_s.shape[2]
+    size = wide_s.shape[3]
     width = rank // group
     count_ex = len_ref.shape[1]
     me = lax.axis_index("par")
@@ -84,7 +84,7 @@
 
     def fetch(l, c):
         span = pl.ds(pl.multiple_of(c * size, size), size)
-        pltpu.make_async_copy(wides[l].at[span, :], wide_s.at[l, c], in_sem.at[l, c, 0]).start()
+        pltpu.make_async_copy(wides[l].at[:, span], wide_s.at[l, c], in_sem.at[l, c, 0]).start()
         pltpu.make_async_copy(narrows[l].at[span, :], narrow_s.at[l, c], in_sem.at[l, c, 1]).start()
 
     for mine in range(LAYERS):
@@ -107,21 +107,13 @@
         pl.semaphore_signal(barrier, inc=1, device_id={"ex": lax.rem(ex + 2 * k, ex_count)}, device_id_type=MESH)
     pl.semaphore_signal(barrier, inc=1, device_id={"ex": sibling}, device_id_type=MESH)
 
-    depth = cbf_ref.shape[1]
-    high = tall.shape[0]
+    depth, deep = cbf_ref.shape[2], cbd_ref.shape[2]
     for l in range(LAYERS):
-        fill = jnp.zeros((depth, rank), jnp.float32)
         for b in range(bf_ref.shape[1]):
-            block = cbf_ref[bf_ref[l, b]].astype(jnp.float32)
-            both = [block, fill] if l == 0 else [fill, block]
-            tall[b * depth:(b + 1) * depth, :] = jnp.concatenate(both, axis=1)
+            tall[:, b * depth:(b + 1) * depth] = cbf_ref[bf_ref[l, b]].astype(jnp.float32)
         pw[l] = tall[...].astype(jnp.bfloat16)
-        deep = cbd_ref.shape[1]
-        fill = jnp.zeros((deep, rank), jnp.float32)
         for b in range(bd_ref.shape[1]):
-            block = cbd_ref[bd_ref[l, b]].astype(jnp.float32)
-            both = [fill, block] if l == 0 else [block, fill]
-            pn[l, b * deep:(b + 1) * deep, :] = jnp.concatenate(both, axis=1).astype(jnp.bfloat16)
+            pn[l, :, b * deep:(b + 1) * deep] = cbd_ref[bd_ref[l, b]]
 
     pl.semaphore_wait(barrier, par_count - 1 + ex_count // 2)
 
@@ -141,11 +133,13 @@
 
     def project(l, c):
         span = pl.ds(0, size)
-        pltpu.make_async_copy(g1_ref.at[span, :], wide_s.at[l, c], in_sem.at[l, c, 0]).wait()
+        pltpu.make_async_copy(g1_ref.at[:, span], wide_s.at[l, c], in_sem.at[l, c, 0]).wait()
         pltpu.make_async_copy(x1_ref.at[span, :], narrow_s.at[l, c], in_sem.at[l, c, 1]).wait()
-        return jnp.dot(wide_s[l, c], pw[l], preferred_element_type=jnp.float32) + jnp.dot(
-            narrow_s[l, c], pn[l], preferred_element_type=jnp.float32
+        first = jnp.dot(pw[l], wide_s[l, c], preferred_element_type=jnp.float32)
+        second = lax.dot_general(
+            pn[l], narrow_s[l, c], (((1,), (1,)), ((), ())), preferred_element_type=jnp.float32
         )
+        return first, second
 
     def partial_copy(step, l, c):
         return pltpu.make_async_remote_copy(
@@ -157,14 +151,18 @@
 
     def send_step(step, carry):
         l, c = order(step)
-        stage[step] = project(l, c).astype(jnp.bfloat16)
+        first, second = project(l, c)
+        stage[step, :rank, :] = first.astype(jnp.bfloat16)
+        stage[step, rank:, :] = second.astype(jnp.bfloat16)
         partial_copy(step, l, c).start()
         return carry
 
     lax.fori_loop(0, sent, send_step, 0)
 
     def keep_step(j, carry):
-        own[j] = project(layer, place * per + j)
+        first, second = project(layer, place * per + j)
+        own[j, :rank, :] = first
+        own[j, rank:, :] = second
         return carry
 
     lax.fori_loop(0, per, keep_step, 0)
@@ -195,14 +193,17 @@
             ).start()
 
     def add_outer(c):
-        held = rows[c]
-        turned[...] = held.astype(jnp.float32).T
         token = lane + c * size
         member = ((token >= starts) & (token < ends)).astype(jnp.float32)
-        slab = turned[pl.ds(pl.multiple_of(place * width, width), width), :]
+        slab = rows[c, pl.ds(pl.multiple_of(layer * rank + place * width, width), width), :].astype(jnp.float32)
         for a in range(width):
             weighted[a * count_ex:(a + 1) * count_ex, :] = (member * slab[a:a + 1, :]).astype(jnp.bfloat16)
-        outer[...] += jnp.dot(weighted[...], held, preferred_element_type=jnp.float32)
+        inside = rows[c, pl.ds(pl.multiple_of((1 - layer) * rank, rank), rank), :]
+        twice[:rank, :] = inside
+        twice[rank:, :] = inside
+        outer[...] += lax.dot_general(
+            weighted[...], twice[...], (((1,), (1,)), ((), ())), preferred_element_type=jnp.float32
+        )
 
     def row_copy(k, j):
         c = place * per + j
@@ -240,9 +241,8 @@
             add_outer(c)
 
     upper = lax.broadcasted_iota(jnp.int32, (count_ex, 2 * rank), 1) >= rank
-    rolled = pltpu.roll(outer[...], rank, 1)
     for pair in range(width // 2):
-        even = rolled[2 * pair * count_ex:(2 * pair + 1) * count_ex, :]
+        even = outer[2 * pair * count_ex:(2 * pair + 1) * count_ex, :]
         odd = outer[(2 * pair + 1) * count_ex:(2 * pair + 2) * count_ex, :]
         grads[:, 2 * rank * pair:2 * rank * (pair + 1)] = jnp.where(upper, odd, even).astype(jnp.bfloat16)
 
@@ -343,16 +343,16 @@
         in_specs=[hbm, hbm, hbm, hbm, vmem, vmem, smem, smem, smem, hbm, vmem],
         out_specs=vmem,
         scratch_shapes=[
-            pltpu.VMEM((LAYERS, chunks, size, broad), bf16),
+            pltpu.VMEM((LAYERS, chunks, broad, size), bf16),
             pltpu.VMEM((LAYERS, chunks, size, slim), bf16),
-            pltpu.VMEM((broad, 2 * rank), f32),
-            pltpu.VMEM((LAYERS, broad, 2 * rank), bf16),
-            pltpu.VMEM((LAYERS, slim, 2 * rank), bf16),
-            pltpu.VMEM((2 * chunks - per, size, 2 * rank), bf16),
-            pltpu.VMEM((par_count, per, size, 2 * rank), bf16),
-            pltpu.VMEM((per, size, 2 * rank), f32),
-            pltpu.VMEM((chunks, size, 2 * rank), bf16),
-            pltpu.VMEM((2 * rank, size), f32),
+            pltpu.VMEM((rank, broad), f32),
+            pltpu.VMEM((LAYERS, rank, broad), bf16),
+            pltpu.VMEM((LAYERS, rank, slim), bf16),
+            pltpu.VMEM((2 * chunks - per, 2 * rank, size), bf16),
+            pltpu.VMEM((par_count, per, 2 * rank, size), bf16),
+            pltpu.VMEM((per, 2 * rank, size), f32),
+            pltpu.VMEM((chunks, 2 * rank, size), bf16),
+            pltpu.VMEM((2 * rank, size), bf16),
             pltpu.VMEM((width * count_ex, size), bf16),
             pltpu.VMEM((width * count_ex, 2 * rank), f32),
             pltpu.VMEM((count_ex, dims), bf16),
@@ -377,7 +377,8 @@
             collective_id=0, has_side_effects=True, vmem_limit_bytes=56 * 1024 * 1024
         ),
     )(
-        x_in1, g_out1, x_in2, g_out2, codebook_d, codebook_f, blocks_d, blocks_f, lengths, bank,
+        x_in1, g_out1.T, x_in2.T, g_out2, codebook_d.transpose(0, 2, 1), codebook_f.transpose(0, 2, 1),
+        blocks_d, blocks_f, lengths, bank,
         query_ids.reshape(1, queries),
     )
 

time: 52.1 us -> 30.4 us (0.58)
  local copies, waits for them, and re-layouts: 22.2 us -> 1.32 us
    unnamed x5 -> x1, local copies, waits for them, and re-layouts: 22.2 us -> 1.32 us
where the time goes in v2:
time: 30.4 us; the launch traced here: 30.1 us
  Pallas kernels  28.8 us (95%)
  local copies, waits for them, and re-layouts  1.32 us (4%)
    pallas_call x1, Pallas kernels, on_device(): pl.pallas_call(functools.partial(kernel, par_count, ex_count, chunks), ou...  28.8 us
    unnamed x1, local copies, waits for them, and re-layouts  1.32 us

profile of v2, /device:TPU:0, one launch (start us, length us, event | category | flops | bytes accessed | tf_op | source)
XLA Modules:
  0.0 30.1 jit_solution(17064404957157539588)
XLA Ops:
  0.0 28.8 %shard_map.109 = f32[16,256]{1,0:T(8,128)} custom-call(bf16[1024,1024]{1,0:T(8,128)(2,1)} %x1_ref.1, bf16[2752,1024]{1,0:T(8,128)(2,1)} %bitcast.5, bf16[2752,1024]{1,0:T(8,128)(2,1)} %bitcast.6, bf16[1024,1024]{1,0:T(8,128)(2,1)} %g2_ref.1, bf16[16,64,128]{2,1,0:T(8,128)(2,1)} %bitcast.8, bf16[16,64,172]{2,1,0:T(8,128)(2,1)} %bitcast.7, s32[2,8]{1,0:T(2,128)} %bd_ref.1, ...), custom_call_target="tpu_custom_call" | custom-call | tf_op jit(solution)/shard_map/pallas_call | solution.py:340
  28.8 1.3 %copy.13 = f32[16,256]{1,0:T(8,128)} copy(f32[16,256]{1,0:T(8,128)} %shard_map.109) | data formatting | bytes 32768

commit v3 on v2

--- a/solution.py
+++ b/solution.py
@@ -76,8 +76,8 @@
         far = step < chunks
         inner = lax.rem(step, chunks)
         l = jnp.where(far, 1 - layer, layer)
-        shift = jnp.where(far, place * per, (place + 1) * per)
-        return l, lax.rem(inner + shift, chunks)
+        spread = lax.rem(inner + place, group) * per + inner // group
+        return l, jnp.where(far, spread, lax.rem(inner + (place + 1) * per, chunks))
 
     wides = (g1_ref, x2_ref)
     narrows = (x1_ref, g2_ref)

time: 30.4 us -> 30.3 us (level)
  no operation moved by 1% of the time
where the time goes in v3:
time: 30.3 us; the launch traced here: 30.1 us
  Pallas kernels  28.8 us (95%)
  local copies, waits for them, and re-layouts  1.32 us (4%)
    pallas_call x1, Pallas kernels, on_device(): pl.pallas_call(functools.partial(kernel, par_count, ex_count, chunks), ou...  28.8 us
    unnamed x1, local copies, waits for them, and re-layouts  1.32 us

profile of v3, /device:TPU:0, one launch (start us, length us, event | category | flops | bytes accessed | tf_op | source)
XLA Modules:
  0.0 30.1 jit_solution(1592375368902468654)
XLA Ops:
  0.0 28.8 %shard_map.109 = f32[16,256]{1,0:T(8,128)} custom-call(bf16[1024,1024]{1,0:T(8,128)(2,1)} %x1_ref.1, bf16[2752,1024]{1,0:T(8,128)(2,1)} %bitcast.5, bf16[2752,1024]{1,0:T(8,128)(2,1)} %bitcast.6, bf16[1024,1024]{1,0:T(8,128)(2,1)} %g2_ref.1, bf16[16,64,128]{2,1,0:T(8,128)(2,1)} %bitcast.8, bf16[16,64,172]{2,1,0:T(8,128)(2,1)} %bitcast.7, s32[2,8]{1,0:T(2,128)} %bd_ref.1, ...), custom_call_target="tpu_custom_call" | custom-call | tf_op jit(solution)/shard_map/pallas_call | solution.py:340
  28.8 1.3 %copy.13 = f32[16,256]{1,0:T(8,128)} copy(f32[16,256]{1,0:T(8,128)} %shard_map.109) | data formatting | bytes 32768
